TPU v7x, 32 devices: a whole 2x2x4 slice. The times are simulated.
32 devices in a mesh: dp: 2 (over core), row: 4 (over z), col: 4 (over y, x).
Axes of the slice: x: 2, y: 2, z: 4, core: 2. Of those that a mesh axis runs over, the one named last changes fastest.
Arguments:
- grad_in: bfloat16 [2, 4096, 16384], P('dp', 'row', 'col'), may hold values from -50 to 50
- grad_out: bfloat16 [2, 16384, 4096], P('dp', 'row', 'col'), may hold values from -50 to 50
- rows_in: float32 [4096], P('row'), may hold values from 0.05 to 0.5
- cols_in: float32 [16384], P('col'), may hold values from 0.05 to 0.5
- rows_out: float32 [16384], P('row'), may hold values from 0.05 to 0.5
- cols_out: float32 [4096], P('col'), may hold values from 0.05 to 0.5
Outputs:
- update_in: float32 [4096, 16384], P('row', 'col')
- update_out: float32 [16384, 4096], P('row', 'col')
- rows_in_new: float32 [4096], P('row')
- cols_in_new: float32 [16384], P('col')
- rows_out_new: float32 [16384], P('row')
- cols_out_new: float32 [4096], P('col')
All inputs are finite; a program needn't handle non-finite values.
Results may differ from a plain program's by a relative error of at most 0.00045.
Values sent between devices are 32-bit elements; how exact they have to be, the bound alone decides.
A program may use at most 128 MiB of HBM per device.

v0:
```python
import jax
import jax.numpy as jnp
from jax import lax
from jax.sharding import PartitionSpec as P

D = 4096
FF = 16384


EPSILON = 1e-30
DECAY = 1.0 - 100.0 ** (-0.8)


def per_device(grad_in, grad_out, rows_in, cols_in, rows_out, cols_out):
    term_in = grad_in[0].astype(jnp.float32)
    term_out = grad_out[0].astype(jnp.float32)
    summed_in, summed_out = lax.psum((term_in, term_out), "dp")
    square_in = summed_in * summed_in + EPSILON
    square_out = summed_out * summed_out + EPSILON
    rowsum_in, rowsum_out = lax.psum(
        (jnp.sum(square_in, axis=1), jnp.sum(square_out, axis=1)), "col"
    )
    colsum_in, colsum_out = lax.psum(
        (jnp.sum(square_in, axis=0), jnp.sum(square_out, axis=0)), "row"
    )
    rows_new_in = DECAY * rows_in + (1.0 - DECAY) * (rowsum_in / FF)
    cols_part_in = DECAY * cols_in + (1.0 - DECAY) * (colsum_in / D)
    rows_new_out = DECAY * rows_out + (1.0 - DECAY) * (rowsum_out / D)
    cols_part_out = DECAY * cols_out + (1.0 - DECAY) * (colsum_out / FF)
    scaled_in = summed_in * lax.rsqrt(rows_new_in)[:, None] * lax.rsqrt(cols_part_in)[None, :]
    scaled_out = summed_out * lax.rsqrt(rows_new_out)[:, None] * lax.rsqrt(cols_part_out)[None, :]
    local = (jnp.sum(scaled_in * scaled_in), jnp.sum(scaled_out * scaled_out))
    energy_in, energy_out = lax.psum((local[0], local[1]), ("row", "col"))
    ratio_in = jnp.sqrt(energy_in / (D * FF))
    ratio_out = jnp.sqrt(energy_out / (D * FF))
    update_in = scaled_in / jnp.maximum(1.0, ratio_in)
    update_out = scaled_out / jnp.maximum(1.0, ratio_out)
    return (update_in, update_out, rows_new_in, cols_part_in, rows_new_out, cols_part_out)


def solution(mesh):
    return jax.shard_map(
        per_device,
        mesh=mesh,
        in_specs=(
            P("dp", "row", "col"),
            P("dp", "row", "col"),
            P("row"),
            P("col"),
            P("row"),
            P("col"),
        ),
        out_specs=(P("row", "col"), P("row", "col"), P("row"), P("col"), P("row"), P("col")),
        check_vma=False,
    )
```

profile of v0, /device:TPU:0, one launch (start us, length us, event | category | flops | bytes accessed | tf_op | source)
XLA Modules:
  0.0 284.2 jit_solution(13869228658963983765)
XLA Ops:
  7.2 0.0 all-reduce.6.cloned.1.call-start
  7.2 11.8 %bitcast_convert_fusion.1 = f32[1024,4096]{1,0:T(8,128)} fusion(bf16[1,1024,4096]{2,1,0:T(8,128)(2,1)} %param.6), kind=kLoop, calls=%fused_computation.13 | loop fusion | flops 4194304 | bytes 25165824 | tf_op jit(solution)/shard_map/convert_element_type | solution.py:15
  19.0 11.7 %bitcast_convert_fusion = f32[4096,1024]{1,0:T(8,128)} fusion(bf16[1,4096,1024]{2,1,0:T(8,128)(2,1)} %param.7), kind=kLoop, calls=%fused_computation.12 | loop fusion | flops 4194304 | bytes 25165824 | tf_op jit(solution)/shard_map/convert_element_type | solution.py:16
  30.7 0.0 all-reduce.6.cloned.1.call-update
  30.8 105.0 %all-reduce.6.cloned.1.call-done = (f32[1024,4096]{1,0:T(8,128)}, f32[4096,1024]{1,0:T(8,128)}) async-done(((f32[1024,4096]{1,0:T(8,128)}, f32[4096,1024]{1,0:T(8,128)}), (f32[1024,4096]{1,0:T(8,128)}, f32[4096,1024]{1,0:T(8,128)})) %all-reduce.6.cloned.1.call-update) | async-done | bytes 33554448 | tf_op jit(solution)/shard_map/psum | solution.py:17
  135.7 0.0 copy-start.2
  135.7 12.7 %fusion.1 = (f32[1024]{0:T(1024)S(1)}, f32[4096]{0:T(1024)S(1)}) fusion(f32[1024,4096]{1,0:T(8,128)} %get-tuple-element.16), kind=kLoop, calls=%fused_computation.7 | loop fusion | flops 16772096 | bytes 16797696 | tf_op jit(solution)/shard_map/reduce_sum | solution.py:21
  148.4 0.0 copy-start.1
  148.4 8.6 %fusion.4 = (f32[4096]{0:T(1024)S(1)}, f32[1024]{0:T(1024)S(1)}) fusion(f32[4096,1024]{1,0:T(8,128)} %get-tuple-element.17), kind=kLoop, calls=%fused_computation.10 | loop fusion | flops 16772096 | bytes 16797696 | tf_op jit(solution)/shard_map/reduce_sum | solution.py:21
  157.0 16.6 %all-reduce.1 = (f32[1024]{0:T(1024)S(1)}, f32[4096]{0:T(1024)S(1)}) all-reduce(f32[1024]{0:T(1024)S(1)} %get-tuple-element.8, f32[4096]{0:T(1024)S(1)} %get-tuple-element.6), channel_id=1, replica_groups=mesh['dp'=2,'row'=4,'col'=4] {'col'}, use_global_device_ids=true, to_apply=%region_2.0 | all-reduce | flops 5120 | bytes 40960 | tf_op jit(solution)/shard_map/psum | solution.py:20
  173.6 0.0 copy-done.2
  173.6 0.6 fusion.8
  174.2 18.9 %all-reduce.2 = (f32[4096]{0:T(1024)S(1)}, f32[1024]{0:T(1024)S(1)}) all-reduce(f32[4096]{0:T(1024)S(1)} %get-tuple-element.9, f32[1024]{0:T(1024)S(1)} %get-tuple-element.7), channel_id=1, replica_groups=mesh['dp'=2,'row'=4,'col'=4] {'row'}, use_global_device_ids=true, to_apply=%region_4.0 | all-reduce | flops 5120 | bytes 40960 | tf_op jit(solution)/shard_map/psum | solution.py:23
  193.1 0.0 copy-done.3
  193.1 0.6 fusion.7
  193.7 0.0 copy-done
  193.7 0.6 fusion.9
  194.3 10.8 %multiply_reduce_fusion.1 = f32[]{:T(128)} fusion(f32[1024,4096]{1,0:T(8,128)} %get-tuple-element.16, f32[4096]{0:T(1024)S(1)} %get-tuple-element.24, f32[1024]{0:T(1024)S(1)} %get-tuple-element.22), kind=kLoop, calls=%fused_computation.3 | loop fusion | flops 16777215 | bytes 16797700 | tf_op jit(solution)/shard_map/reduce_sum | solution.py:32
  205.1 0.0 copy-done.1
  205.1 0.6 fusion.6
  205.7 8.9 %multiply_reduce_fusion = f32[]{:T(128)} fusion(f32[4096,1024]{1,0:T(8,128)} %get-tuple-element.17, f32[1024]{0:T(1024)S(1)} %get-tuple-element.20, f32[4096]{0:T(1024)S(1)} %get-tuple-element.18), kind=kLoop, calls=%fused_computation | loop fusion | flops 16777215 | bytes 16797700 | tf_op jit(solution)/shard_map/reduce_sum | solution.py:32
  214.6 37.2 %all-reduce = (f32[]{:T(128)}, f32[]{:T(128)}) all-reduce(f32[]{:T(128)} %multiply_reduce_fusion.1, f32[]{:T(128)} %multiply_reduce_fusion), channel_id=1, replica_groups=mesh['dp'=2,'row'=4,'col'=4] {'row','col'}, use_global_device_ids=true, to_apply=%region_6.0 | all-reduce | flops 2 | bytes 16 | tf_op jit(solution)/shard_map/psum | solution.py:33
  253.2 12.2 %fusion.2 = f32[1024,4096]{1,0:T(8,128)} fusion(f32[1024,4096]{1,0:T(8,128)} %get-tuple-element.16, f32[]{:T(128)S(6)} %max.6, f32[4096]{0:T(1024)S(1)} %get-tuple-element.24, f32[1024]{0:T(1024)S(1)} %get-tuple-element.22), kind=kLoop, calls=%fused_computation.8 | loop fusion | flops 12582912 | bytes 33574916 | tf_op jit(solution)/shard_map/div | solution.py:36
  265.4 11.9 %fusion.5 = f32[4096,1024]{1,0:T(8,128)} fusion(f32[4096,1024]{1,0:T(8,128)} %get-tuple-element.17, f32[]{:T(128)S(6)} %max.7, f32[1024]{0:T(1024)S(1)} %get-tuple-element.20, f32[4096]{0:T(1024)S(1)} %get-tuple-element.18), kind=kLoop, calls=%fused_computation.11 | loop fusion | flops 12582912 | bytes 33574916 | tf_op jit(solution)/shard_map/div | solution.py:37
  (2 shorter events, 0.0 us)
Async XLA Ops:
  7.2 128.6 %all-reduce.6.cloned.1.call-start = ((), (), s32[]{:S(2)}) async-start(), calls=%async_computation | async-start | bytes 67108864 | tf_op jit(solution)/shard_map/psum | solution.py:17
  135.7 37.8 %copy-start.2 = (f32[1024]{0:T(1024)S(1)}, f32[1024]{0:T(1024)}, u32[]{:S(2)}) copy-start(f32[1024]{0:T(1024)} %param.8) | copy-start | bytes 12292
  135.7 57.4 %copy-start.3 = (f32[1024]{0:T(1024)S(1)}, f32[1024]{0:T(1024)}, u32[]{:S(2)}) copy-start(f32[1024]{0:T(1024)} %param.11) | copy-start | bytes 12292
  135.7 58.0 %copy-start = (f32[4096]{0:T(1024)S(1)}, f32[4096]{0:T(1024)}, u32[]{:S(2)}) copy-start(f32[4096]{0:T(1024)} %param.9) | copy-start | bytes 49156
  148.4 56.7 %copy-start.1 = (f32[4096]{0:T(1024)S(1)}, f32[4096]{0:T(1024)}, u32[]{:S(2)}) copy-start(f32[4096]{0:T(1024)} %param.10) | copy-start | bytes 49156
Sparse Core Ops, SparseCore 0:
  30.9 104.7 all-reduce.5
where the time goes:
time: 285 us; the launch traced here: 284 us
  waiting for transfers between devices  105 us (37%)
  other arithmetic  91 us (32%)
  blocking collectives  72.7 us (26%)
  between operations  15.4 us (5%)
    psum x1, waiting for transfers between devices, per_device(): summed_in, summed_out = lax.psum((term_in, term_out), 'dp')  105 us
    psum x1, blocking collectives, per_device(): energy_in, energy_out = lax.psum((local[0], local[1]), ('row', 'col'))  37.2 us
    reduce_sum x2, other arithmetic, per_device(): local = (jnp.sum(scaled_in * scaled_in), jnp.sum(scaled_out * scaled_out))  19.7 us
    psum x1, blocking collectives, per_device(): lax.psum((jnp.sum(square_in, axis=0), jnp.sum(square_out, axis=0)), 'row')  18.9 us
    psum x1, blocking collectives, per_device(): lax.psum((jnp.sum(square_in, axis=1), jnp.sum(square_out, axis=1)), 'col')  16.6 us
    reduce_sum x1, other arithmetic, per_device(): jnp.sum(square_in, axis=1)  12.7 us
    div x1, other arithmetic, per_device(): update_in = scaled_in / jnp.maximum(1.0, ratio_in)  12.2 us
    div x1, other arithmetic, per_device(): update_out = scaled_out / jnp.maximum(1.0, ratio_out)  11.9 us
  transfers between devices with their start and end apart: 1, of which 1 were waited for; matrix products, arithmetic and copies ran while one was open for 0% of the time, Pallas kernels for 0%

commit v1 on v0

v1 whole, which is shorter than its diff:
```python
import functools
import jax
import jax.numpy as jnp
from jax import lax
from jax.experimental import pallas as pl
from jax.experimental.pallas import tpu as pltpu
from jax.sharding import PartitionSpec as P

EPSILON = 1e-30
DECAY = 1.0 - 100.0 ** (-0.8)
MESH = pl.DeviceIdType.MESH
F32 = jnp.float32
CHUNKS = 8
SLOTS = 3
LAG = 3


def kernel(nr, nc, g_in, g_out, rows_in, cols_in, rows_out, cols_out,
           acc_in, acc_out, rnew_in, cnew_in, rnew_out, cnew_out, rf_in, cf_in, rf_out, cf_out,
           own_in, own_out, oth_in, oth_out, stage_in, stage_out, rowp_in, rowp_out, colp_in, colp_out,
           rrep_in, rrep_out, rowsend, rowrecv, colsend, colrecv, esend, erecv, fsend, frecv,
           own_sem, oth_sem, rs_send, rs_recv, ag_send, ag_recv,
           row_s, row_r, col_s, col_r, e_s, e_r, f_s, f_r):
    d, r, c = lax.axis_index("dp"), lax.axis_index("row"), lax.axis_index("col")
    partner = (1 - d, r, c)
    ncol, nrow = 2 * nc, 2 * nr
    my_col, my_row = d * nc + c, d * nr + r

    def col_peer(q):
        p = lax.rem(my_col + q, ncol)
        return (p // nc, r, lax.rem(p, nc))

    def row_peer(q):
        p = lax.rem(my_row + q, nrow)
        return (p // nr, lax.rem(p, nr), c)

    grads, accs = (g_in, g_out), (acc_in, acc_out)
    owns, oths, stages = (own_in, own_out), (oth_in, oth_out), (stage_in, stage_out)
    rowps, colps, rreps = (rowp_in, rowp_out), (colp_in, colp_out), (rrep_in, rrep_out)
    halves = [a.shape[0] // 2 for a in accs]
    chs = [h // CHUNKS for h in halves]
    widths = [a.shape[1] for a in accs]
    tasks = [(m, k) for m in range(2) for k in range(CHUNKS)]
    n = len(tasks)

    def rows_of(m, k, who):
        return pl.ds(pl.multiple_of(who * halves[m] + k * chs[m], chs[m]), chs[m])

    loads_own, loads_oth = [], []
    for t, (m, k) in enumerate(tasks):
        loads_oth.append(pltpu.make_async_copy(
            grads[m].at[0, rows_of(m, k, 1 - d), :], oths[m].at[pl.ds(k * chs[m], chs[m]), :], oth_sem.at[t]))
        loads_own.append(pltpu.make_async_copy(
            grads[m].at[0, rows_of(m, k, d), :], owns[m].at[pl.ds(k * chs[m], chs[m]), :], own_sem.at[t]))
    for t in range(n):
        loads_oth[t].start()
        loads_own[t].start()

    barrier = pltpu.get_barrier_semaphore()
    for q in range(1, ncol):
        pl.semaphore_signal(barrier, inc=1, device_id=col_peer(q), device_id_type=MESH)
    for q in range(1, nrow):
        pl.semaphore_signal(barrier, inc=1, device_id=row_peer(q), device_id_type=MESH)
    for m in range(2):
        colps[m][...] = jnp.zeros_like(colps[m])
    rowsend[...] = jnp.zeros_like(rowsend)
    pl.semaphore_wait(barrier, ncol + nrow - 2)

    rs, rs_in, ag, ag_in = [], [], [], []
    for t, (m, k) in enumerate(tasks):
        rs.append(pltpu.make_async_remote_copy(
            src_ref=stages[m].at[k % SLOTS], dst_ref=accs[m].at[rows_of(m, k, 1 - d), :],
            send_sem=rs_send.at[t], recv_sem=rs_recv.at[t], device_id=partner, device_id_type=MESH))
        rs_in.append(pltpu.make_async_remote_copy(
            src_ref=stages[m].at[k % SLOTS], dst_ref=accs[m].at[rows_of(m, k, d), :],
            send_sem=rs_send.at[t], recv_sem=rs_recv.at[t], device_id=partner, device_id_type=MESH))
        ag.append(pltpu.make_async_remote_copy(
            src_ref=accs[m].at[rows_of(m, k, d), :], dst_ref=accs[m].at[rows_of(m, k, d), :],
            send_sem=ag_send.at[t], recv_sem=ag_recv.at[t], device_id=partner, device_id_type=MESH))
        ag_in.append(pltpu.make_async_remote_copy(
            src_ref=accs[m].at[rows_of(m, k, 1 - d), :], dst_ref=accs[m].at[rows_of(m, k, 1 - d), :],
            send_sem=ag_send.at[t], recv_sem=ag_recv.at[t], device_id=partner, device_id_type=MESH))

    def send(t):
        m, k = tasks[t]
        if k >= SLOTS:
            rs[t - SLOTS].wait_send()
        loads_oth[t].wait()

        @pl.loop(0, chs[m] // 16)
        def _(i):
            at = pl.multiple_of(i * 16, 16)
            src = pl.multiple_of(k * chs[m] + i * 16, 16)
            stages[m][k % SLOTS, pl.ds(at, 16), :] = oths[m][pl.ds(src, 16), :].astype(F32)

        rs[t].start()

    def take(t):
        m, k = tasks[t]
        loads_own[t].wait()
        rs_in[t].wait_recv()
        step = min(1024, widths[m])

        @pl.loop(0, chs[m] // 16)
        def _(i):
            at = pl.multiple_of(k * chs[m] + i * 16, 16)
            there = pl.multiple_of(d * halves[m] + k * chs[m] + i * 16, 16)
            part = jnp.zeros((16, 128), F32)
            for b in range(0, widths[m], step):
                s = accs[m][pl.ds(there, 16), b:b + step] + owns[m][pl.ds(at, 16), b:b + step].astype(F32)
                accs[m][pl.ds(there, 16), b:b + step] = s
                sq = s * s + EPSILON
                colps[m][:, b:b + step] += sq[:8] + sq[8:]
                for j in range(0, step, 128):
                    part = part + sq[:, j:j + 128]
            rowps[m][pl.ds(at, 16), :] = part

    for t in range(n):
        send(t)
        if t >= LAG:
            take(t - LAG)
    for t in range(n - LAG):
        ag[t].start()
    for t in range(n - LAG, n):
        take(t)
        ag[t].start()

    nbs = [h // 128 for h in halves]
    offs = [0, (nbs[0] + 7) // 8 * 8]
    for m in range(2):
        for b in range(nbs[m]):
            rowsend[offs[m] + b:offs[m] + b + 1, :] = jnp.sum(
                rowps[m][b * 128:(b + 1) * 128, :].T, axis=0, keepdims=True)
    colsend[:, :widths[0]] = jnp.sum(colp_in[...], axis=0, keepdims=True)
    colsend[:, widths[0]:] = jnp.sum(colp_out[...], axis=0, keepdims=True)

    def exchange(src, dst, me, count, peer, ssem, rsem):
        copies = []
        for q in range(1, count):
            copies.append((pltpu.make_async_remote_copy(
                src_ref=src, dst_ref=dst.at[me], send_sem=ssem.at[q], recv_sem=rsem.at[q],
                device_id=peer(q), device_id_type=MESH),
                pltpu.make_async_remote_copy(
                src_ref=src, dst_ref=dst.at[lax.rem(me + count - q, count)], send_sem=ssem.at[q],
                recv_sem=rsem.at[q], device_id=peer(q), device_id_type=MESH)))
        for out, _ in copies:
            out.start()
        dst[me] = src[...]
        return copies

    def finish(copies):
        for out, into in copies:
            into.wait_recv()
            out.wait_send()

    row_copies = exchange(rowsend, rowrecv, my_col, ncol, col_peer, row_s, row_r)
    col_copies = exchange(colsend, colrecv, my_row, nrow, row_peer, col_s, col_r)
    finish(row_copies)
    finish(col_copies)

    fulls = [(widths[m] * nc, accs[m].shape[0] * nr) for m in range(2)]
    for m, (old, new, rf) in enumerate(((rows_in, rnew_in, rf_in), (rows_out, rnew_out, rf_out))):
        for h in range(2):
            total = rowrecv[h * nc, offs[m]:offs[m] + nbs[m], :]
            for j in range(1, nc):
                total = total + rowrecv[h * nc + j, offs[m]:offs[m] + nbs[m], :]
            fresh = DECAY * old[h * nbs[m]:(h + 1) * nbs[m], :] + (1.0 - DECAY) * (total / fulls[m][0])
            new[h * nbs[m]:(h + 1) * nbs[m], :] = fresh
            rf[h * nbs[m]:(h + 1) * nbs[m], :] = lax.rsqrt(fresh)
    csum = colrecv[0]
    for j in range(1, nrow):
        csum = csum + colrecv[j]
    for m, (old, new, cf) in enumerate(((cols_in, cnew_in, cf_in), (cols_out, cnew_out, cf_out))):
        total = csum[:, :widths[0]] if m == 0 else csum[:, widths[0]:]
        fresh = DECAY * old[...] + (1.0 - DECAY) * (total / fulls[m][1])
        new[...] = fresh
        cf[...] = lax.rsqrt(fresh)

    for m, (rf, cf) in enumerate(((rf_in, cf_in), (rf_out, cf_out))):
        for b in range(nbs[m]):
            line = rf[pl.ds(d * nbs[m] + b, 1), :]
            rreps[m][b * 128:(b + 1) * 128, :] = jnp.broadcast_to(line, (128, 128)).T

        def body(i, total):
            at = pl.multiple_of(i * 16, 16)
            there = pl.multiple_of(d * halves[m] + i * 16, 16)
            factor = rreps[m][pl.ds(at, 16), :]
            for j in range(0, widths[m], 128):
                x = accs[m][pl.ds(there, 16), j:j + 128] * factor * cf[:, j:j + 128]
                total = total + x * x
            return total

        energy = lax.fori_loop(0, halves[m] // 16, body, jnp.zeros((16, 128), F32))
        esend[m * 8:(m + 1) * 8, :] = energy[:8] + energy[8:]

    finish(exchange(esend, erecv, my_col, ncol, col_peer, e_s, e_r))
    total = erecv[0]
    for j in range(1, ncol):
        total = total + erecv[j]
    fsend[...] = total

    def ring_peer(q):
        return (d, lax.rem(r + q, nr), c)

    finish(exchange(fsend, frecv, r, nr, ring_peer, f_s, f_r))
    total = frecv[0]
    for j in range(1, nr):
        total = total + frecv[j]
    for m, rf in enumerate((rf_in, rf_out)):
        mean = jnp.sum(total[m * 8:(m + 1) * 8, :], keepdims=True) / (float(fulls[m][0]) * fulls[m][1])
        rf[...] = rf[...] * (1.0 / jnp.maximum(1.0, jnp.sqrt(mean)))

    for t, (m, k) in enumerate(tasks):
        if k >= CHUNKS - SLOTS:
            rs[t].wait_send()
        ag_in[t].wait_recv()
        ag[t].wait_send()


def fused(nr, nc, grad_in, grad_out, rows_in, cols_in, rows_out, cols_out):
    (ri, ci), (ro, co) = grad_in.shape[1:], grad_out.shape[1:]
    hi, ho = ri // 2, ro // 2
    nb = (hi // 128 + 7) // 8 * 8 + (ho // 128 + 7) // 8 * 8
    vm = pl.BlockSpec(memory_space=pltpu.VMEM)
    small = lambda *s: jax.ShapeDtypeStruct(s, F32)
    dma = lambda k: pltpu.SemaphoreType.DMA((k,))
    n = 2 * CHUNKS
    vmem = lambda *s: pltpu.VMEM(s, F32)
    outs = pl.pallas_call(
        functools.partial(kernel, nr, nc),
        out_shape=(
            pltpu.VMEM((ri, ci), F32), pltpu.VMEM((ro, co), F32),
            small(ri // 128, 128), small(1, ci), small(ro // 128, 128), small(1, co),
            small(ri // 128, 128), small(1, ci), small(ro // 128, 128), small(1, co),
        ),
        in_specs=[pl.BlockSpec(memory_space=pl.ANY)] * 2 + [vm] * 4,
        out_specs=(vm,) * 10,
        scratch_shapes=[
            pltpu.VMEM((hi, ci), jnp.bfloat16), pltpu.VMEM((ho, co), jnp.bfloat16),
            pltpu.VMEM((hi, ci), jnp.bfloat16), pltpu.VMEM((ho, co), jnp.bfloat16),
            vmem(SLOTS, hi // CHUNKS, ci), vmem(SLOTS, ho // CHUNKS, co),
            vmem(hi, 128), vmem(ho, 128), vmem(8, ci), vmem(8, co),
            vmem(hi, 128), vmem(ho, 128),
            vmem(nb, 128), vmem(2 * nc, nb, 128),
            vmem(1, ci + co), vmem(2 * nr, 1, ci + co),
            vmem(16, 128), vmem(2 * nc, 16, 128), vmem(16, 128), vmem(nr, 16, 128),
            dma(n), dma(n), dma(n), dma(n), dma(n), dma(n),
            dma(2 * nc), dma(2 * nc), dma(2 * nr), dma(2 * nr),
            dma(2 * nc), dma(2 * nc), dma(nr), dma(nr),
        ],
        compiler_params=pltpu.CompilerParams(
            collective_id=0, has_side_effects=True, vmem_limit_bytes=VMEM_LIMIT),
    )(grad_in, grad_out, rows_in.reshape(-1, 128), cols_in.reshape(1, -1),
      rows_out.reshape(-1, 128), cols_out.reshape(1, -1))
    s_in, s_out, rn_in, cn_in, rn_out, cn_out, rf_in, cf_in, rf_out, cf_out = outs
    update_in = s_in * rf_in.reshape(-1)[:, None] * cf_in
    update_out = s_out * rf_out.reshape(-1)[:, None] * cf_out
    return (update_in, update_out, rn_in.reshape(-1), cn_in.reshape(-1), rn_out.reshape(-1), cn_out.reshape(-1))


VMEM_LIMIT = 29 * 1024 * 1024


def plain(nr, nc, grad_in, grad_out, rows_in, cols_in, rows_out, cols_out):
    def one(grad, rows, cols):
        height, width = grad.shape[1] * nr, grad.shape[2] * nc
        summed = lax.psum(grad[0].astype(F32), "dp")
        square = summed * summed + EPSILON
        rows_new = DECAY * rows + (1.0 - DECAY) * (lax.psum(jnp.sum(square, axis=1), "col") / width)
        cols_new = DECAY * cols + (1.0 - DECAY) * (lax.psum(jnp.sum(square, axis=0), "row") / height)
        scaled = summed * lax.rsqrt(rows_new)[:, None] * lax.rsqrt(cols_new)[None, :]
        energy = lax.psum(jnp.sum(scaled * scaled), ("row", "col"))
        ratio = jnp.sqrt(energy / (float(height) * width))
        return scaled / jnp.maximum(1.0, ratio), rows_new, cols_new

    u_in, r_in, c_in = one(grad_in, rows_in, cols_in)
    u_out, r_out, c_out = one(grad_out, rows_out, cols_out)
    return (u_in, u_out, r_in, c_in, r_out, c_out)


def solution(mesh):
    nr, nc = mesh.shape["row"], mesh.shape["col"]

    def per_device(grad_in, grad_out, *factors):
        whole = all(g.shape[1] % (256 * CHUNKS // 4) == 0 and g.shape[2] % 1024 == 0 for g in (grad_in, grad_out))
        return (fused if whole else plain)(nr, nc, grad_in, grad_out, *factors)

    return jax.shard_map(
        per_device,
        mesh=mesh,
        in_specs=(P("dp", "row", "col"), P("dp", "row", "col"), P("row"), P("col"), P("row"), P("col")),
        out_specs=(P("row", "col"), P("row", "col"), P("row"), P("col"), P("row"), P("col")),
        check_vma=False,
    )
```

time: 285 us -> 85.6 us (0.30)
  waiting for transfers between devices: 105 us -> 0 us
  other arithmetic: 91 us -> 13.9 us
  blocking collectives: 72.7 us -> 0 us
  Pallas kernels: 0 us -> 68.3 us
  between operations: 15.4 us -> 0.69 us
    psum x1 -> x0, waiting for transfers between devices: 105 us -> none  [per_device(): summed_in, summed_out = lax.psum((term_in, term_out), 'dp')]
    psum x3 -> x0, blocking collectives: 72.7 us -> none  [the longest x1 37.2 us: per_device(): energy_in, energy_out = lax.psum((local[0], local[1]), ('row', 'col'))]
    pallas_call x0 -> x1, Pallas kernels: none -> 68.3 us  [fused(): pl.pallas_call(functools.partial(kernel, nr, nc), out_shape=(pltpu.VMEM((...]
    reduce_sum x4 -> x0, other arithmetic: 40.9 us -> none  [the longest x2 19.7 us: per_device(): local = (jnp.sum(scaled_in * scaled_in), jnp.sum(scaled_out * scaled_out))]
    div x2 -> x0, other arithmetic: 24.1 us -> none  [the longest x1 12.2 us: per_device(): update_in = scaled_in / jnp.maximum(1.0, ratio_in)]
    convert_element_type x2 -> x0, other arithmetic: 23.5 us -> none  [the longest x1 11.8 us: per_device(): term_in = grad_in[0].astype(jnp.float32)]
    mul x0 -> x2, other arithmetic: none -> 13.9 us  [the longest x1 7.52 us: fused(): update_in = s_in * rf_in.reshape(-1)[:, None] * cf_in]
  transfers between devices with their start and end apart: 1 -> 0, of which waited for: 1 -> 0; matrix products, arithmetic and copies ran while one was open for 0% -> 0% of each run, Pallas kernels for 0% -> 0%
where the time goes in v1:
time: 85.6 us; the launch traced here: 85.2 us
  Pallas kernels  68.3 us (80%)
  other arithmetic  13.9 us (16%)
  local copies, waits for them, and re-layouts  2.43 us (3%)
    pallas_call x1, Pallas kernels, fused(): pl.pallas_call(functools.partial(kernel, nr, nc), out_shape=(pltpu.VMEM((...  68.3 us
    mul x1, other arithmetic, fused(): update_in = s_in * rf_in.reshape(-1)[:, None] * cf_in  7.52 us
    mul x1, other arithmetic, fused(): update_out = s_out * rf_out.reshape(-1)[:, None] * cf_out  6.34 us
    unnamed x16, local copies, waits for them, and re-layouts  2.43 us

profile of v1, /device:TPU:0, one launch (start us, length us, event | category | flops | bytes accessed | tf_op | source)
XLA Modules:
  0.0 85.2 jit_solution(421194917052621550)
XLA Ops:
  0.6 68.3 %shard_map.109 = (f32[1024,4096]{1,0:T(8,128)S(1)}, f32[4096,1024]{1,0:T(8,128)S(1)}, f32[8,128]{1,0:T(8,128)}, f32[1,4096]{1,0:T(1,128)}, f32[32,128]{1,0:T(8,1...) custom-call(bf16[1,1024,4096]{2,1,0:T(8,128)(2,1)} %g_in.1, ...), custom_call_target="tpu_custom_call" | custom-call | tf_op jit(solution)/shard_map/pallas_call | solution.py:229
  68.9 0.0 copy-start
  68.9 0.0 copy-start.3
  68.9 7.5 %multiply_multiply_fusion.1 = f32[1024,4096]{1,0:T(8,128)} fusion(f32[1024,4096]{1,0:T(8,128)S(1)} %get-tuple-element.16, f32[4096]{0:T(1024)} %bitcast.13, f32[1024]{0:T(1024)} %bitcast.19), kind=kLoop, calls=%fused_computation.1 | loop fusion | flops 8388608 | bytes 33574912 | tf_op jit(solution)/shard_map/mul | solution.py:256
  76.4 0.0 copy-done
  76.4 0.0 copy-done.3
  76.4 0.0 copy-start.5
  76.4 0.0 copy-start.2
  76.5 0.0 copy-start.1
  76.5 0.0 copy-start.4
  76.5 6.3 %multiply_multiply_fusion = f32[4096,1024]{1,0:T(8,128)} fusion(f32[4096,1024]{1,0:T(8,128)S(1)} %get-tuple-element.19, f32[1024]{0:T(1024)S(1)} %bitcast.18, f32[4096]{0:T(1024)S(1)} %bitcast.12), kind=kLoop, calls=%fused_computation | loop fusion | flops 8388608 | bytes 33574912 | tf_op jit(solution)/shard_map/mul | solution.py:257
  82.8 0.0 copy-done.5
  82.8 0.6 copy.16
  83.4 0.0 copy-done.2
  83.4 0.6 copy.17
  84.0 0.0 copy-done.1
  84.0 0.6 copy.18
  84.6 0.0 copy-done.4
  84.6 0.6 copy.19
Async XLA Ops:
  68.9 7.5 %copy-start = (f32[32,128]{1,0:T(8,128)S(1)}, f32[32,128]{1,0:T(8,128)}, u32[]{:S(2)}) copy-start(f32[32,128]{1,0:T(8,128)} %get-tuple-element.20) | copy-start | bytes 49156
  68.9 7.5 %copy-start.3 = (f32[1,1024]{1,0:T(1,128)S(1)}, f32[1,1024]{1,0:T(1,128)}, u32[]{:S(2)}) copy-start(f32[1,1024]{1,0:T(1,128)} %get-tuple-element.21) | copy-start | bytes 12292
  76.4 6.4 %copy-start.5 = (f32[8,128]{1,0:T(8,128)S(1)}, f32[8,128]{1,0:T(8,128)}, u32[]{:S(2)}) copy-start(f32[8,128]{1,0:T(8,128)} %get-tuple-element.22) | copy-start | bytes 12292
  76.4 7.0 %copy-start.2 = (f32[1,4096]{1,0:T(1,128)S(1)}, f32[1,4096]{1,0:T(1,128)}, u32[]{:S(2)}) copy-start(f32[1,4096]{1,0:T(1,128)} %get-tuple-element.23) | copy-start | bytes 49156
  76.5 7.6 %copy-start.1 = (f32[32,128]{1,0:T(8,128)S(1)}, f32[32,128]{1,0:T(8,128)}, u32[]{:S(2)}) copy-start(f32[32,128]{1,0:T(8,128)} %get-tuple-element.24) | copy-start | bytes 49156
  76.5 8.2 %copy-start.4 = (f32[1,1024]{1,0:T(1,128)S(1)}, f32[1,1024]{1,0:T(1,128)}, u32[]{:S(2)}) copy-start(f32[1,1024]{1,0:T(1,128)} %get-tuple-element.25) | copy-start | bytes 12292
